TPU v7x, 128 devices: a whole 4x4x4 slice. The times are simulated.
128 devices in a mesh: dp: 16 (over y, z), tensor: 8 (over x, core).
Axes of the slice: x: 4, y: 4, z: 4, core: 2. Of those that a mesh axis runs over, the one named last changes fastest.
Arguments:
- hidden_in: bfloat16 [9216, 8192], P(('dp', 'tensor')), may hold values from -600 to 600
- norm_gain: float32 [8192], replicated, may hold values from 0.1 to 1.9
- query_weight: bfloat16 [8192, 4096], P('dp', 'tensor'), may hold values from -0.0625 to 0.0625
- keyval_weight: bfloat16 [8192, 2, 1024], P('dp', None, 'tensor'), may hold values from -0.0625 to 0.0625
- query_bias: float32 [4096], P('tensor'), may hold values from -40 to 40
- keyval_bias: float32 [2, 1024], P(None, 'tensor'), may hold values from -40 to 40
- out_weight: bfloat16 [4096, 8192], P('tensor', 'dp'), may hold values from -0.09375 to 0.09375
- bundle_row_lengths: int32 [16], replicated, may hold values from 1 to 72, as said below
- move_plan: int32 [16], replicated, may hold values from 0 to 15, each once
- first_len: int32 [16, 16], replicated, may hold values from 1 to 72, as said below
Outputs:
- attended: bfloat16 [9216, 8192], P(('dp', 'tensor'))
Inputs may be any that keep to these rules, and one draw needn't show every extreme that they name: `bundle_row_lengths`: the lengths sum to 576; exactly one of them is 72. `move_plan`: each value appears once. first_len[h, b] is at least 1 and at most bundle_row_lengths[b].
All inputs are finite; a program needn't handle non-finite values.
Results may differ from a plain program's by a relative error of at most 0.024.
Values may be sent and summed in bfloat16 or wider, within the bound.
No kernel may reach another device: no remote copies, remote signals or barrier semaphores. Data moves between devices by JAX's collectives and lax.ppermute only.
A program may use at most 128 MiB of HBM per device.

v0:
```python
import jax
import jax.numpy as jnp
from jax import lax
from jax.sharding import PartitionSpec as P

HD = 128


THETA = 1000000.0
EPS = 1e-06


def rotate_heads(values, places):
    half_dim = values.shape[-1] // 2
    indices = jnp.arange(half_dim, dtype=jnp.float32)
    frequency = THETA ** (-2.0 * indices / values.shape[-1])
    angles = places[:, None] * frequency[None, :]
    cosines = jnp.cos(angles)[:, None, :]
    sine_vals = jnp.sin(angles)[:, None, :]
    lower_half = values[..., :half_dim]
    upper_half = values[..., half_dim:]
    return jnp.concatenate(
        [
            lower_half * cosines - upper_half * sine_vals,
            upper_half * cosines + lower_half * sine_vals,
        ],
        axis=-1,
    )


def document_layout(bundle_row_lengths, first_row, row_count):
    offsets = jnp.cumsum(bundle_row_lengths) - bundle_row_lengths
    places = jnp.arange(row_count, dtype=jnp.int32)
    bundle_id = jnp.sum((places[:, None] >= offsets[None, :]).astype(jnp.int32), axis=1) - 1
    selector = (
        bundle_id[:, None] == jnp.arange(offsets.shape[0], dtype=jnp.int32)[None, :]
    ).astype(jnp.int32)
    starts = jnp.sum(selector * offsets[None, :], axis=1)
    splits = jnp.sum(selector * first_row[None, :], axis=1)
    second = (places - starts >= splits).astype(jnp.int32)
    segment = bundle_id * 2 + second
    doc_start = starts + second * splits
    return (segment, (places - doc_start).astype(jnp.float32), starts, bundle_id)


def normalize(rows, norm_gain):
    values = rows.astype(jnp.float32)
    scale = lax.rsqrt(jnp.mean(values * values, axis=1, keepdims=True) + EPS)
    return (values * scale * norm_gain).astype(jnp.bfloat16)


def attend(grouped, key_heads, value_heads, segment):
    row_count = grouped.shape[0]
    attention_scores = jnp.einsum(
        "rkgd,skd->kgrs", grouped, key_heads, preferred_element_type=jnp.float32
    ) * grouped.shape[-1] ** (-0.5)
    places = jnp.arange(row_count, dtype=jnp.int32)
    allowed = (segment[:, None] == segment[None, :]) & (places[None, :] <= places[:, None])
    attention_scores = jnp.where(allowed[None, None], attention_scores, -jnp.inf)
    highest = jnp.max(attention_scores, axis=-1, keepdims=True)
    exponent = jnp.exp(attention_scores - highest)
    weights = (exponent / jnp.sum(exponent, axis=-1, keepdims=True)).astype(jnp.bfloat16)
    context = jnp.einsum("kgrs,skd->rkgd", weights, value_heads, preferred_element_type=jnp.float32)
    return context.astype(jnp.bfloat16)


def shards(
    hidden_in,
    norm_gain,
    query_weight,
    keyval_weight,
    query_bias,
    keyval_bias,
    out_weight,
    bundle_row_lengths,
    move_plan,
    first_len,
):
    dp_count = lax.axis_size("dp")
    dp_rank = lax.axis_index("dp")
    groups = lax.axis_size("tensor")
    tok_dev = hidden_in.shape[0]
    row_count = tok_dev * groups
    capacity = 2 * row_count // dp_count
    bundle_ids = jnp.arange(move_plan.shape[0], dtype=jnp.int32)
    slot_ids = jnp.arange(dp_count, dtype=jnp.int32)
    lane_ids = jnp.arange(capacity, dtype=jnp.int32)
    offsets = jnp.cumsum(bundle_row_lengths) - bundle_row_lengths
    sources = (dp_rank - move_plan) % dp_count
    dest_first = jnp.sum(
        first_len * (slot_ids[:, None] == sources[None, :]).astype(jnp.int32), axis=0
    )
    outgoing = (move_plan[None, :] == ((slot_ids - dp_rank) % dp_count)[:, None]).astype(jnp.int32)
    send_start = jnp.sum(outgoing * offsets[None, :], axis=1)
    send_length = jnp.sum(outgoing * bundle_row_lengths[None, :], axis=1)
    send_live = lane_ids[None, :] < send_length[:, None]
    send_rows = jnp.where(send_live, send_start[:, None] + lane_ids[None, :], 0).reshape(-1)
    dest_segment, dest_position, dest_starts, dest_bundle = document_layout(
        bundle_row_lengths, dest_first, row_count
    )
    arrival = jnp.sum(
        (dest_bundle[:, None] == bundle_ids[None, :]).astype(jnp.int32) * sources[None, :], axis=1
    )
    receive_rows = arrival * capacity + jnp.arange(row_count, dtype=jnp.int32) - dest_starts
    combined = jnp.concatenate(
        [query_weight, keyval_weight.reshape(keyval_weight.shape[0], -1)], axis=1
    )
    query_cols = query_weight.shape[1]
    kv_cols = keyval_weight.shape[2]
    columns = lax.all_to_all(hidden_in, "tensor", split_axis=1, concat_axis=0, tiled=True)
    picked = jnp.take(columns, send_rows, axis=0)
    picked = jnp.where(send_live.reshape(-1, 1), picked, jnp.zeros((), columns.dtype))
    received = lax.all_to_all(
        picked.reshape(dp_count, capacity, columns.shape[1]),
        "dp",
        split_axis=0,
        concat_axis=0,
        tiled=True,
    )
    moved_rows = jnp.take(
        received.reshape(dp_count * capacity, received.shape[2]), receive_rows, axis=0
    )
    gathered = lax.all_gather(moved_rows, "tensor", axis=1, tiled=True)
    normed = normalize(gathered, norm_gain)
    columns = normed
    projected = jnp.dot(
        columns,
        lax.all_gather(combined, "dp", axis=0, tiled=True),
        preferred_element_type=jnp.float32,
    )
    rows_here = normed.shape[0]
    query_heads = rotate_heads(
        (projected[:, :query_cols] + query_bias).reshape(rows_here, -1, HD), dest_position
    )
    key_heads = rotate_heads(
        (projected[:, query_cols : query_cols + kv_cols] + keyval_bias[0]).reshape(
            rows_here, -1, HD
        ),
        dest_position,
    )
    value_heads = projected[:, query_cols + kv_cols :] + keyval_bias[1]
    arrived = jnp.concatenate(
        [
            query_heads.reshape(rows_here, -1).astype(jnp.bfloat16),
            key_heads.reshape(rows_here, -1).astype(jnp.bfloat16),
            value_heads.astype(jnp.bfloat16),
        ],
        axis=1,
    )
    heads_here = query_cols // HD
    kv_here = kv_cols // HD
    grouped = arrived[:, :query_cols].reshape(row_count, kv_here, heads_here // kv_here, HD)
    key_heads = arrived[:, query_cols : query_cols + kv_cols].reshape(row_count, kv_here, HD)
    value_heads = arrived[:, query_cols + kv_cols :].reshape(row_count, kv_here, HD)
    context = attend(grouped, key_heads, value_heads, dest_segment).reshape(row_count, query_cols)
    partial_out = jnp.dot(
        context,
        lax.all_gather(out_weight, "dp", axis=1, tiled=True),
        preferred_element_type=jnp.float32,
    )
    return lax.psum_scatter(
        partial_out.astype(jnp.bfloat16), "tensor", scatter_dimension=0, tiled=True
    )


def solution(mesh):
    in_specs = (
        P(("dp", "tensor"), None),
        P(),
        P("dp", "tensor"),
        P("dp", None, "tensor"),
        P("tensor"),
        P(None, "tensor"),
        P("tensor", "dp"),
        P(),
        P(),
        P(),
    )
    out_specs = P(("dp", "tensor"), None)
    return jax.shard_map(shards, mesh=mesh, in_specs=in_specs, out_specs=out_specs, check_vma=False)
```

profile of v0, /device:TPU:1, one launch (start us, length us, event | category | flops | bytes accessed | tf_op | source)
XLA Modules:
  0.0 380.6 jit_solution(14251803318119991510)
XLA Ops:
  6.5 2.4 copy.44
  8.9 5.8 %all-to-all-start = ((bf16[72,8,1024]{2,0,1:T(8,128)(2,1)}), bf16[72,8,1024]{2,0,1:T(8,128)(2,1)S(1)}, u32[]{:S(2)}, u32[]{:S(2)}) async-start(bf16[72,8,1024]{2,0,1:T(8,128)(2,1)} %bitcast.66), calls=%async_computation | async-start | bytes 2359296 | tf_op jit(solution)/shard_map/all_to_all | solution.py:110
  15.0 0.5 and_select_fusion
  16.0 15.2 %all-to-all-done = bf16[72,8,1024]{2,0,1:T(8,128)(2,1)S(1)} async-done(((bf16[72,8,1024]{2,0,1:T(8,128)(2,1)}), bf16[72,8,1024]{2,0,1:T(8,128)(2,1)S(1)}, u32[]{:S(2)}, u32[]{:S(2)}) %all-to-all-start) | async-done | bytes 1179680 | tf_op jit(solution)/shard_map/all_to_all | solution.py:110
  31.2 4.4 %gather_fusion = bf16[1152,1024]{1,0:T(8,128)(2,1)S(1)} fusion(bf16[576,1024]{1,0:T(8,128)(2,1)S(1)} %bitcast.68, s32[2048]{0:T(1024)S(1)} %pad_clamp_fusion), kind=kCustom, calls=%fused_computation | custom fusion | bytes 4723200 | tf_op jit(solution)/shard_map/jit(_take)/gather | solution.py:111
  35.6 1.7 select_select_fusion
  37.3 7.9 %all-to-all-start.1 = ((bf16[16,72,1024]{2,1,0:T(8,128)(2,1)}), bf16[16,72,1024]{2,1,0:T(8,128)(2,1)S(1)}, u32[]{:S(2)}, u32[]{:S(2)}) async-start(bf16[16,72,1024]{2,1,0:T(8,128)(2,1)} %select_select_fusion), calls=%async_computation.1 | async-start | bytes 4718592 | tf_op jit(solution)/shard_map/all_to_all | solution.py:113
  45.5 0.5 compare_and_fusion.1
  46.1 29.6 %all-to-all-done.1 = bf16[16,72,1024]{2,1,0:T(8,128)(2,1)S(1)} async-done(((bf16[16,72,1024]{2,1,0:T(8,128)(2,1)}), bf16[16,72,1024]{2,1,0:T(8,128)(2,1)S(1)}, u32[]{:S(2)}, u32[]{:S(2)}) %all-to-all-start.1) | async-done | bytes 2359328 | tf_op jit(solution)/shard_map/all_to_all | solution.py:113
  75.7 2.9 gather_fusion.1
  78.6 1.9 broadcast_select_fusion
  80.6 0.9 pad_maximum_fusion
  81.6 0.7 all-gather.8.cloned.1.call-update
  82.4 0.3 fusion.11
  82.6 1.1 multiply_cosine_fusion
  83.7 50.8 %all-gather.4.cloned.1.call-done = bf16[576,8192]{1,0:T(8,128)(2,1)} async-done(((bf16[576,1024]{1,0:T(8,128)(2,1)}), bf16[576,8192]{1,0:T(8,128)(2,1)}) %all-gather.4.cloned.1.call-update) | async-done | bytes 9437200 | tf_op jit(solution)/shard_map/all_gather | solution.py:123
  134.5 5.6 %fusion = f32[576]{0:T(1024)S(1)} fusion(bf16[576,8192]{1,0:T(8,128)(2,1)} %all-gather.4.cloned.1.call-done), kind=kLoop, calls=%fused_computation.4 | loop fusion | flops 14155200 | bytes 9439488 | tf_op jit(solution)/shard_map/reduce_sum | solution.py:48
  140.2 86.6 %all-gather.6.cloned.1.call-done = bf16[8192,768]{1,0:T(8,128)(2,1)} async-done(((bf16[512,768]{1,0:T(8,128)(2,1)}), bf16[8192,768]{1,0:T(8,128)(2,1)}) %all-gather.6.cloned.1.call-update) | async-done | bytes 12582928 | tf_op jit(solution)/shard_map/all_gather | solution.py:128
  226.7 13.2 %fusion.3 = f32[576,768]{1,0:T(8,128)S(1)} fusion(bf16[8192,768]{1,0:T(8,128)(2,1)} %all-gather.6.cloned.1.call-done, bf16[576,8192]{1,0:T(8,128)(2,1)} %all-gather.4.cloned.1.call-done, f32[8192]{0:T(1024)S(1)} %copy-done.11, f32[576]{0:T(1024)S(1)} %add_rsqrt_fusion), kind=kOutput, calls=%fused_computation.8 | convolution fusion | flops 7266631680 | bytes 23824640 | tf_op jit(solution)/shard_map/dot_general | solution.py:126
  239.9 1.2 copy-done
  241.3 0.4 reshape.423
  241.7 1.0 fusion.32
  242.7 1.4 fusion.40
  244.1 0.7 fusion.50
  244.8 0.3 subtract_convert_fusion
  245.1 1.6 fusion.8
  246.7 1.3 fusion.7
  248.0 2.9 fusion.15
  251.0 0.5 copy.27
  251.4 54.7 %all-gather.8.cloned.1.call-done = bf16[512,8192]{1,0:T(8,128)(2,1)} async-done(((bf16[512,512]{1,0:T(8,128)(2,1)}), bf16[512,8192]{1,0:T(8,128)(2,1)}) %all-gather.8.cloned.1.call-update) | async-done | bytes 8388624 | tf_op jit(solution)/shard_map/all_gather | solution.py:158
  306.1 10.8 %convolution_convert_fusion = bf16[576,8192]{1,0:T(8,128)(2,1)} fusion(bf16[512,8192]{1,0:T(8,128)(2,1)} %all-gather.8.cloned.1.call-done, bf16[72,8,4,128]{3,2,1,0:T(4,128)(2,1)S(1)} %bitcast.73), kind=kOutput, calls=%fused_computation.7 | convolution fusion | flops 4836556800 | bytes 18415616 | tf_op jit(solution)/shard_map/dot_general | solution.py:156
  317.0 57.1 %reduce-scatter.2.cloned.1.call-done = bf16[72,8192]{1,0:T(8,128)(2,1)} async-done(((bf16[576,8192]{1,0:T(8,128)(2,1)}), bf16[72,8192]{1,0:T(8,128)(2,1)}) %reduce-scatter.2.cloned.1.call-update) | async-done | bytes 1179664 | tf_op jit(solution)/shard_map/reduce_scatter | solution.py:161
  (53 shorter events, 1.4 us)
Async XLA Ops:
  6.5 8.2 %copy-start.7 = (s32[16]{0:T(128)S(1)}, s32[16]{0:T(128)}, u32[]{:S(2)}) copy-start(s32[16]{0:T(128)} %param.17) | copy-start | bytes 196
  6.5 8.5 %copy-start.8 = (s32[16]{0:T(128)S(1)}, s32[16]{0:T(128)}, u32[]{:S(2)}) copy-start(s32[16]{0:T(128)} %param.18) | copy-start | bytes 196
  8.9 22.3 %all-to-all-start = ((bf16[72,8,1024]{2,0,1:T(8,128)(2,1)}), bf16[72,8,1024]{2,0,1:T(8,128)(2,1)S(1)}, u32[]{:S(2)}, u32[]{:S(2)}) async-start(bf16[72,8,1024]{2,0,1:T(8,128)(2,1)} %bitcast.66), calls=%async_computation | async-start | bytes 2359296 | tf_op jit(solution)/shard_map/all_to_all | solution.py:110
  15.0 0.7 copy-start.4
  37.3 8.0 %copy-start.3 = (s32[16,16]{1,0:T(8,128)S(1)}, s32[16,16]{1,0:T(8,128)}, u32[]{:S(2)}) copy-start(s32[16,16]{1,0:T(8,128)} %param.19) | copy-start | bytes 3076
  37.3 8.0 %copy-start.6 = (s32[16]{0:T(128)S(1)}, s32[16]{0:T(128)}, u32[]{:S(2)}) copy-start(s32[16]{0:T(128)} %get-tuple-element.27) | copy-start | bytes 196
  37.3 8.0 %copy-start.5 = (s32[16]{0:T(128)S(1)}, s32[16]{0:T(128)}, u32[]{:S(2)}) copy-start(s32[16]{0:T(128)} %copy-done.4) | copy-start | bytes 196
  37.3 38.4 %all-to-all-start.1 = ((bf16[16,72,1024]{2,1,0:T(8,128)(2,1)}), bf16[16,72,1024]{2,1,0:T(8,128)(2,1)S(1)}, u32[]{:S(2)}, u32[]{:S(2)}) async-start(bf16[16,72,1024]{2,1,0:T(8,128)(2,1)} %select_select_fusion), calls=%async_computation.1 | async-start | bytes 4718592 | tf_op jit(solution)/shard_map/all_to_all | solution.py:113
  45.2 89.3 %all-gather.4.cloned.1.call-start = ((), (), s32[]{:S(2)}) async-start(), calls=%async_computation.3 | async-start | bytes 10616832 | tf_op jit(solution)/shard_map/all_gather | solution.py:123
  78.5 2.0 copy-start.2
  78.5 2.0 copy-start.1
  80.4 1.9 copy-start.10
  80.4 146.3 %all-gather.6.cloned.1.call-start = ((), (), s32[]{:S(2)}) async-start(), calls=%async_computation.4 | async-start | bytes 13369344 | tf_op jit(solution)/shard_map/all_gather | solution.py:128
  81.5 224.6 %all-gather.8.cloned.1.call-start = ((), (), s32[]{:S(2)}) async-start(), calls=%async_computation.5 | async-start | bytes 8912896 | tf_op jit(solution)/shard_map/all_gather | solution.py:158
  82.3 291.8 %reduce-scatter.2.cloned.1.call-start = ((), (), s32[]{:S(2)}) async-start(), calls=%async_computation.6 | async-start | bytes 10616832 | tf_op jit(solution)/shard_map/reduce_scatter | solution.py:161
  83.7 143.0 %copy-start.11 = (f32[8192]{0:T(1024)S(1)}, f32[8192]{0:T(1024)}, u32[]{:S(2)}) copy-start(f32[8192]{0:T(1024)} %param.11) | copy-start | bytes 98308
  140.1 101.0 %copy-start.9 = (f32[512]{0:T(512)S(1)}, f32[512]{0:T(512)}, u32[]{:S(2)}) copy-start(f32[512]{0:T(512)} %param.14) | copy-start | bytes 6148
  239.9 1.2 copy-start
Sparse Core Ops, SparseCore 0:
  80.6 53.9 all-gather.3
  136.7 89.9 all-gather.5
  228.9 77.2 all-gather.7
  317.1 56.9 reduce-scatter.1
where the time goes:
time: 381 us
  waiting for transfers between devices  295 us (77%)
  matrix products  28.5 us (7%)
  other arithmetic  17.4 us (5%)
  starting transfers between devices  13.9 us (4%)
  between operations  13.4 us (4%)
  local copies, waits for them, and re-layouts  12.6 us (3%)
    all_gather x1, waiting for transfers between devices, shards(): lax.all_gather(combined, 'dp', axis=0, tiled=True)  86.6 us
    reduce_scatter x1, waiting for transfers between devices, shards(): lax.psum_scatter(partial_out.astype(jnp.bfloat16), 'tensor', scatter_dime...  57.1 us
    all_gather x1, waiting for transfers between devices, shards(): lax.all_gather(out_weight, 'dp', axis=1, tiled=True)  54.7 us
    all_gather x1, waiting for transfers between devices, shards(): gathered = lax.all_gather(moved_rows, 'tensor', axis=1, tiled=True)  50.8 us
    all_to_all x1, waiting for transfers between devices, shards(): lax.all_to_all(picked.reshape(dp_count, capacity, columns.shape[1]), 'dp'...  29.6 us
    all_to_all x1, waiting for transfers between devices, shards(): lax.all_to_all(hidden_in, 'tensor', split_axis=1, concat_axis=0, tiled=True)  15.2 us
    dot_general x1, matrix products, shards(): jnp.dot(columns, lax.all_gather(combined, 'dp', axis=0, tiled=True), pref...  13.2 us
    dot_general x1, matrix products, shards(): jnp.dot(context, lax.all_gather(out_weight, 'dp', axis=1, tiled=True), pr...  10.8 us
  transfers between devices with their start and end apart: 6, of which 6 were waited for; matrix products, arithmetic and copies ran while one was open for 9% of the time, Pallas kernels for 0%

commit v1 on v0

v1 whole, which is shorter than its diff:
```python
import jax
import jax.numpy as jnp
from jax import lax
from jax.sharding import Mesh, PartitionSpec as P

HD = 128
THETA = 1000000.0
EPS = 1e-06
BF = jnp.bfloat16
F32 = jnp.float32
DP = ("y", "z")


def ring(n, step):
    return [(i, (i + step) % n) for i in range(n)]


def hop(v, step):
    return lax.ppermute(v, "x", ring(lax.axis_size("x"), step))


def swap(v):
    return lax.ppermute(v, "c", [(0, 1), (1, 0)])


def dot(a, b):
    return jnp.dot(a, b, preferred_element_type=F32)


def rotate(values, cosines, sines):
    rows = values.shape[0]
    heads = values.reshape(rows, -1, HD)
    lower, upper = heads[..., : HD // 2], heads[..., HD // 2 :]
    cosines, sines = cosines[:, None, :], sines[:, None, :]
    turned = jnp.concatenate(
        [lower * cosines - upper * sines, upper * cosines + lower * sines], axis=-1
    )
    return turned.astype(BF)


def attend(queries, keys, values, allowed):
    scores = jnp.einsum("rgd,sd->grs", queries, keys, preferred_element_type=F32) * HD ** (-0.5)
    scores = jnp.where(allowed[None], scores, -jnp.inf)
    exponent = jnp.exp(scores - jnp.max(scores, axis=-1, keepdims=True))
    probs = (exponent / jnp.sum(exponent, axis=-1, keepdims=True)).astype(BF)
    context = jnp.einsum("grs,sd->rgd", probs, values, preferred_element_type=F32)
    return context.astype(BF)


def shards(
    hidden_in,
    norm_gain,
    query_weight,
    keyval_weight,
    query_bias,
    keyval_bias,
    out_weight,
    lengths,
    move_plan,
    first_len,
):
    packs = lax.axis_size(DP)
    pack = lax.axis_index(DP)
    x = lax.axis_index("x")
    core = lax.axis_index("c")
    nx = lax.axis_size("x")
    here = hidden_in.shape[0]
    width = hidden_in.shape[1]
    rows = here * nx * 2
    q_cols = query_weight.shape[1]

    combined = jnp.concatenate([query_weight, keyval_weight.reshape(keyval_weight.shape[0], -1)], axis=1)
    w_in = lax.all_gather(combined, DP, axis=0, tiled=True)

    values = hidden_in.astype(F32)
    scale = lax.rsqrt(jnp.mean(values * values, axis=1, keepdims=True) + EPS)
    own = (values * scale * norm_gain).astype(BF)
    half = width // 2
    left = hop(own, 1)
    right = hop(own, -1)
    far = jnp.concatenate([hop(left[:, :half], 1), hop(right[:, half:], -1)], axis=1)
    parts = []
    for part in (own, left, far, right):
        parts += [part, swap(part)]
    normed = jnp.concatenate(parts, axis=0)
    r = jnp.arange(here, dtype=jnp.int32)
    places = jnp.concatenate(
        [
            here * (2 * ((x - s) % nx) + (core if k == 0 else 1 - core)) + r
            for s in range(4)
            for k in range(2)
        ]
    )

    places_out = jnp.concatenate(
        [here * (2 * ((x - s) % nx) + k) + r for s in range(4) for k in range(2)]
    )

    ids = jnp.arange(lengths.shape[0], dtype=jnp.int32)
    offsets = jnp.cumsum(lengths) - lengths
    bundle = jnp.sum((places[:, None] >= offsets[None, :]).astype(jnp.int32), axis=1) - 1
    selector = (bundle[:, None] == ids[None, :]).astype(jnp.int32)
    starts = jnp.sum(selector * offsets[None, :], axis=1)
    first_here = jnp.sum(first_len * (jnp.arange(packs)[:, None] == pack).astype(jnp.int32), axis=0)
    splits = jnp.sum(selector * first_here[None, :], axis=1)
    second = (places - starts >= splits).astype(jnp.int32)
    segment = bundle * 2 + second
    position = (places - starts - second * splits).astype(F32)
    allowed = (segment[:, None] == segment[None, :]) & (places[None, :] <= places[:, None])
    indices = jnp.arange(HD // 2, dtype=F32)
    angles = position[:, None] * (THETA ** (-2.0 * indices / HD))[None, :]
    cosines, sines = jnp.cos(angles), jnp.sin(angles)

    cols = out_weight.shape[1] // 2
    w_low, w_high = out_weight[:, :cols], out_weight[:, cols:]
    mine = jnp.where(core == 0, w_low, w_high)
    other = swap(jnp.where(core == 0, w_high, w_low))
    w_both = jnp.concatenate([mine, other], axis=0)
    w_both, left_tie = lax.optimization_barrier((w_both, left))
    chunks = 2
    step = cols // chunks
    w_out = [
        lax.all_gather(w_both[:, j * step : (j + 1) * step], DP, axis=0, tiled=False)
        for j in range(chunks)
    ]

    projected = dot(normed, w_in)
    queries = rotate(projected[:, :q_cols] + query_bias, cosines, sines)
    keys = rotate(projected[:, q_cols : q_cols + HD] + keyval_bias[0], cosines, sines)[:, 0]
    vals = (projected[:, q_cols + HD :] + keyval_bias[1]).astype(BF)
    context = attend(queries, keys, vals, allowed).reshape(rows, q_cols)

    capacity = 2 * rows // packs
    lanes = jnp.arange(capacity, dtype=jnp.int32)
    slots = jnp.arange(packs, dtype=jnp.int32)
    outgoing = (move_plan[None, :] == ((slots - pack) % packs)[:, None]).astype(jnp.int32)
    send_start = jnp.sum(outgoing * offsets[None, :], axis=1)
    send_length = jnp.sum(outgoing * lengths[None, :], axis=1)
    live = lanes[None, :] < send_length[:, None]
    send_rows = jnp.where(live, send_start[:, None] + lanes[None, :], -1).reshape(-1)
    pick = (send_rows[:, None] == places[None, :]).astype(BF)
    sent = dot(pick, context).astype(BF).reshape(packs, capacity, q_cols)
    got = lax.all_to_all(sent, DP, split_axis=0, concat_axis=0, tiled=True)
    sources = (pack - move_plan) % packs
    bundle_out = jnp.sum((places_out[:, None] >= offsets[None, :]).astype(jnp.int32), axis=1) - 1
    selector = (bundle_out[:, None] == ids[None, :]).astype(jnp.int32)
    source = jnp.sum(selector * sources[None, :], axis=1)
    slot = source * capacity + places_out - jnp.sum(selector * offsets[None, :], axis=1)
    place = (slot[:, None] == jnp.arange(packs * capacity, dtype=jnp.int32)[None, :]).astype(BF)
    moved = dot(place, got.reshape(packs * capacity, q_cols)).astype(BF)
    both = jnp.concatenate([moved, swap(moved)], axis=1)

    outs = []
    block = 2 * here
    for j in range(chunks):
        partial = jnp.concatenate([dot(both, w_out[j][d]).astype(BF) for d in range(packs)], axis=1)
        part = [partial[s * block : (s + 1) * block] for s in range(4)]
        mid = part[0].shape[1] // 2
        a = hop(part[2][:, :mid], 1)
        b = hop(part[2][:, mid:], -1)
        up = jnp.concatenate(
            [(part[3][:, :mid].astype(F32) + a.astype(F32)).astype(BF), part[3][:, mid:]], axis=1
        )
        down = jnp.concatenate(
            [part[1][:, :mid], (part[1][:, mid:].astype(F32) + b.astype(F32)).astype(BF)], axis=1
        )
        u, v = hop(up, 1), hop(down, -1)
        total = (part[0].astype(F32) + u.astype(F32) + v.astype(F32)).astype(BF)
        mine = jnp.where(core == 0, total[:here], total[here:])
        other = swap(jnp.where(core == 0, total[here:], total[:here]))
        mine, other = mine.reshape(here, packs, 1, step), other.reshape(here, packs, 1, step)
        outs.append(
            jnp.concatenate(
                [jnp.where(core == 0, mine, other), jnp.where(core == 0, other, mine)], axis=2
            )
        )
    out = jnp.stack(outs, axis=3)
    return out.reshape(here, width)


def solution(mesh):
    packs, tensor = mesh.devices.shape
    side = int(round(packs**0.5))
    fine = Mesh(mesh.devices.reshape(side, packs // side, tensor // 2, 2), ("y", "z", "x", "c"))
    every = ("y", "z", "x", "c")
    heads = ("x", "c")
    in_specs = (
        P(every, None),
        P(),
        P(DP, heads),
        P(DP, None, heads),
        P(heads),
        P(None, heads),
        P(heads, DP),
        P(),
        P(),
        P(),
    )
    return jax.shard_map(
        shards, mesh=fine, in_specs=in_specs, out_specs=P(every, None), check_vma=False
    )
```

time: 381 us -> 283 us (0.74)
  waiting for transfers between devices: 295 us -> 147 us
  starting transfers between devices: 13.9 us -> 36.6 us
  matrix products: 28.5 us -> 48.3 us
  local copies, waits for them, and re-layouts: 12.6 us -> 23.6 us
  other arithmetic: 17.4 us -> 13.1 us
    all_gather x3, waiting for transfers between devices: 192 us -> 45.8 us  [the longest x2 37.7 us: shards(): lax.all_gather(w_both[:, j * step:(j + 1) * step], DP, axis=0, tiled=False)]
    ppermute x0 -> x20, waiting for transfers between devices: none -> 74.1 us  [the longest x12 71.7 us: hop(): return lax.ppermute(v, 'x', ring(lax.axis_size('x'), step))]
    reduce_scatter x1 -> x0, waiting for transfers between devices: 57.1 us -> none  [shards(): lax.psum_scatter(partial_out.astype(jnp.bfloat16), 'tensor', scatter_dime...]
    ppermute x0 -> x20, starting transfers between devices: none -> 31.3 us  [the longest x12 17.6 us: hop(): return lax.ppermute(v, 'x', ring(lax.axis_size('x'), step))]
    all_to_all x2 -> x1, waiting for transfers between devices: 44.8 us -> 26.8 us  [shards(): got = lax.all_to_all(sent, DP, split_axis=0, concat_axis=0, tiled=True)]
    dot_general x4 -> x36, matrix products: 28.5 us -> 43.3 us  [the longest x35 39.3 us: dot(): return jnp.dot(a, b, preferred_element_type=F32)]
    unnamed x25 -> x64, local copies, waits for them, and re-layouts: 1.3 us -> 12.5 us
    all_to_all x2 -> x1, starting transfers between devices: 13.7 us -> 5.23 us  [shards(): got = lax.all_to_all(sent, DP, split_axis=0, concat_axis=0, tiled=True)]
  transfers between devices with their start and end apart: 6 -> 24, of which waited for: 6 -> 15; matrix products, arithmetic and copies ran while one was open for 9% -> 27% of each run, Pallas kernels for 0% -> 0%
where the time goes in v1:
time: 283 us; the launch traced here: 282 us
  waiting for transfers between devices  147 us (52%)
  matrix products  48.3 us (17%)
  starting transfers between devices  36.6 us (13%)
  local copies, waits for them, and re-layouts  23.6 us (8%)
  between operations  13.9 us (5%)
  other arithmetic  13.1 us (5%)
    ppermute x12, waiting for transfers between devices, hop(): return lax.ppermute(v, 'x', ring(lax.axis_size('x'), step))  71.7 us
    dot_general x35, matrix products, dot(): return jnp.dot(a, b, preferred_element_type=F32)  39.3 us
    all_gather x2, waiting for transfers between devices, shards(): lax.all_gather(w_both[:, j * step:(j + 1) * step], DP, axis=0, tiled=False)  37.7 us
    all_to_all x1, waiting for transfers between devices, shards(): got = lax.all_to_all(sent, DP, split_axis=0, concat_axis=0, tiled=True)  26.8 us
    ppermute x12, starting transfers between devices, hop(): return lax.ppermute(v, 'x', ring(lax.axis_size('x'), step))  17.6 us
    ppermute x8, starting transfers between devices, swap(): return lax.ppermute(v, 'c', [(0, 1), (1, 0)])  13.7 us
    unnamed x64, local copies, waits for them, and re-layouts  12.5 us
    all_gather x1, waiting for transfers between devices, shards(): w_in = lax.all_gather(combined, DP, axis=0, tiled=True)  8.05 us
  transfers between devices with their start and end apart: 24, of which 15 were waited for; matrix products, arithmetic and copies ran while one was open for 27% of the time, Pallas kernels for 0%

profile of v1, /device:TPU:1, one launch (start us, length us, event | category | flops | bytes accessed | tf_op | source)
XLA Modules:
  0.0 282.3 jit_solution(2139323204201403666)
XLA Ops:
  7.6 2.0 pad_maximum_fusion.3
  10.1 1.8 constant_dynamic-update-slice_fusion.7
  11.9 2.0 collective-permute-start.1
  16.2 24.5 %collective-permute-done.1 = bf16[72,8192]{1,0:T(8,128)(2,1)S(1)} collective-permute-done((bf16[72,8192]{1,0:T(8,128)(2,1)}, bf16[72,8192]{1,0:T(8,128)(2,1)S(1)}, u32[]{:S(2)}, u32[]{:S(2)}) %collective-permute-start.1) | collective-permute-done | bytes 1179680 | tf_op jit(solution)/shard_map/ppermute | solution.py:19
  49.0 1.9 multiply_cosine_fusion
  51.8 19.4 %collective-permute-done.4 = bf16[72,8192]{1,0:T(8,128)(2,1)S(1)} collective-permute-done((bf16[72,8192]{1,0:T(8,128)(2,1)}, bf16[72,8192]{1,0:T(8,128)(2,1)S(1)}, u32[]{:S(2)}, u32[]{:S(2)}) %collective-permute-start.4) | collective-permute-done | bytes 1179680 | tf_op jit(solution)/shard_map/ppermute | solution.py:19
  72.1 2.7 collective-permute-start.5
  76.0 2.4 constant_dynamic-update-slice_fusion.6
  79.5 7.5 %collective-permute-done.5 = bf16[72,4096]{1,0:T(8,128)(2,1)S(1)} collective-permute-done((bf16[72,4096]{1,0:T(8,128)(2,1)}, bf16[72,4096]{1,0:T(8,128)(2,1)S(1)}, u32[]{:S(2)}, u32[]{:S(2)}) %collective-permute-start.5) | collective-permute-done | bytes 589856 | tf_op jit(solution)/shard_map/ppermute | solution.py:19
  87.1 1.9 collective-permute-start.6
  95.1 8.1 %all-gather.6.cloned.1.call-done = bf16[8192,768]{1,0:T(8,128)(2,1)} async-done(((bf16[512,768]{1,0:T(8,128)(2,1)}), bf16[8192,768]{1,0:T(8,128)(2,1)}) %all-gather.6.cloned.1.call-update) | async-done | bytes 12582928 | tf_op jit(solution)/shard_map/all_gather | solution.py:73
  103.2 13.0 %fusion.87 = f32[576,768]{1,0:T(8,128)S(1)} fusion(bf16[576,8192]{1,0:T(8,128)(2,1)} %constant_dynamic-update-slice_fusion, bf16[8192,768]{1,0:T(8,128)(2,1)} %all-gather.6.cloned.1.call-done), kind=kOutput, calls=%fused_computation.280 | convolution fusion | flops 7247757312 | bytes 23789568 | tf_op jit(solution)/shard_map/dot_general | solution.py:27
  121.1 4.9 %fusion.86 = (f32[4,576]{1,0:T(4,128)S(1)}, f32[4,576,576]{1,2,0:T(8,128)}) fusion(pred[576,576]{0,1:T(8,128)(4,1)S(1)} %copy-done.5, bf16[576,4,64]{2,0,1:T(8,128)(2,1)S(1)} %get-tuple-element.17, bf16[576,4,64]{2,0,1:T(8,128)(2,1)S(1)} %get-tuple-element.16, bf16[576,64]{1,0:T(8,128)(2,1)S(1)} %get-tuple-element.37, ...), kind=kOutput, calls=%fused_computation.279 | convolution fusion | flops 346522176 | bytes 6386688 | tf_op jit(solution)/shard_map/sub | solution.py:44
  126.1 4.0 %fusion.16 = bf16[4,72,8,128]{3,2,1,0:T(8,128)(2,1)S(1)} fusion(f32[4,576,576]{1,2,0:T(8,128)} %get-tuple-element.109, f32[4,576]{1,0:T(4,128)S(1)} %get-tuple-element.108, f32[576,768]{1,0:T(8,128)} %copy-done.1, f32[128]{0:T(128)S(1)} %copy-done.18), kind=kOutput, calls=%fused_computation.24 | convolution fusion | flops 342835200 | bytes 6792704 | tf_op jit(solution)/shard_map/grs,sd->rgd/dot_general | solution.py:46
  130.1 2.1 convolution_convert_fusion
  132.3 5.2 %all-to-all-start = ((bf16[16,72,512]{2,1,0:T(8,128)(2,1)}), bf16[16,72,512]{2,1,0:T(8,128)(2,1)S(1)}, u32[]{:S(2)}, u32[]{:S(2)}) async-start(bf16[16,72,512]{2,1,0:T(8,128)(2,1)} %bitcast.10), calls=%async_computation | async-start | bytes 2359296 | tf_op jit(solution)/shard_map/all_to_all | solution.py:143
  137.6 26.8 %all-to-all-done = bf16[16,72,512]{2,1,0:T(8,128)(2,1)S(1)} async-done(((bf16[16,72,512]{2,1,0:T(8,128)(2,1)}), bf16[16,72,512]{2,1,0:T(8,128)(2,1)S(1)}, u32[]{:S(2)}, u32[]{:S(2)}) %all-to-all-start) | async-done | bytes 1179680 | tf_op jit(solution)/shard_map/all_to_all | solution.py:143
  165.4 2.5 collective-permute-start.8
  186.4 36.3 %all-gather.10.cloned.1.call-done = bf16[16384,128]{1,0:T(8,128)(2,1)} async-done(((bf16[1024,128]{1,0:T(8,128)(2,1)}), bf16[16384,128]{1,0:T(8,128)(2,1)}) %all-gather.10.cloned.1.call-update) | async-done | bytes 4194320 | tf_op jit(solution)/shard_map/all_gather | solution.py:123
  222.7 1.9 constant_dynamic-update-slice_fusion.55
  224.6 1.9 constant_dynamic-update-slice_fusion.54
  235.6 1.8 collective-permute-start.17
  237.7 2.7 collective-permute-start.13
  240.7 2.8 collective-permute-done.17
  243.6 2.8 collective-permute-start.18
  246.3 6.0 %collective-permute-done.11 = bf16[144,2048]{1,0:T(8,128)(2,1)S(1)} collective-permute-done((bf16[144,2048]{1,0:T(8,128)(2,1)S(1)}, bf16[144,2048]{1,0:T(8,128)(2,1)S(1)}, u32[]{:S(2)}, u32[]{:S(2)}) %collective-permute-start.11) | collective-permute-done | bytes 589856 | tf_op jit(solution)/shard_map/ppermute | solution.py:19
  252.4 3.7 %collective-permute-done.13 = bf16[144,2048]{1,0:T(8,128)(2,1)S(1)} collective-permute-done((bf16[144,2048]{1,0:T(8,128)(2,1)S(1)}, bf16[144,2048]{1,0:T(8,128)(2,1)S(1)}, u32[]{:S(2)}, u32[]{:S(2)}) %collective-permute-start.13) | collective-permute-done | bytes 589856 | tf_op jit(solution)/shard_map/ppermute | solution.py:19
  257.5 3.4 %collective-permute-start.14 = (bf16[72,2048]{1,0:T(8,128)(2,1)S(1)}, bf16[72,2048]{1,0:T(8,128)(2,1)S(1)}, u32[]{:S(2)}, u32[]{:S(2)}) collective-permute-start(bf16[72,2048]{1,0:T(8,128)(2,1)S(1)} %broadcast_select_fusion.2), channel_id=1, source_target_pairs={{0,1},{1,0},{2,3},{3,2},{4,5},{5,4},{6,7},{7,6},{8,9},{9,8},{10,11... | collective-permute-start | bytes 884744 | tf_op jit(solution)/shard_map/ppermute | solution.py:23
  260.9 4.1 %collective-permute-done.16 = bf16[144,2048]{1,0:T(8,128)(2,1)S(1)} collective-permute-done((bf16[144,2048]{1,0:T(8,128)(2,1)S(1)}, bf16[144,2048]{1,0:T(8,128)(2,1)S(1)}, u32[]{:S(2)}, u32[]{:S(2)}) %collective-permute-start.16) | collective-permute-done | bytes 589856 | tf_op jit(solution)/shard_map/ppermute | solution.py:19
  265.0 3.7 %collective-permute-done.18 = bf16[144,2048]{1,0:T(8,128)(2,1)S(1)} collective-permute-done((bf16[144,2048]{1,0:T(8,128)(2,1)S(1)}, bf16[144,2048]{1,0:T(8,128)(2,1)S(1)}, u32[]{:S(2)}, u32[]{:S(2)}) %collective-permute-start.18) | collective-permute-done | bytes 589856 | tf_op jit(solution)/shard_map/ppermute | solution.py:19
  269.0 1.9 collective-permute-start.19
  273.8 1.9 reshape.603
  (191 shorter events, 60.4 us)
Async XLA Ops:
  6.5 96.6 %all-gather.6.cloned.1.call-start = ((), (), s32[]{:S(2)}) async-start(), calls=%async_computation.1 | async-start | bytes 13369344 | tf_op jit(solution)/shard_map/all_gather | solution.py:73
  9.7 159.7 %all-gather.8.cloned.1.call-start = ((), (), s32[]{:S(2)}) async-start(), calls=%async_computation.2 | async-start | bytes 4456448 | tf_op jit(solution)/shard_map/all_gather | solution.py:123
  11.9 28.9 %collective-permute-start.1 = (bf16[72,8192]{1,0:T(8,128)(2,1)}, bf16[72,8192]{1,0:T(8,128)(2,1)S(1)}, u32[]{:S(2)}, u32[]{:S(2)}) collective-permute-start(bf16[72,8192]{1,0:T(8,128)(2,1)} %get-tuple-element.15), channel_id=1, source_target_pairs={{0,2},{2,4},{4,6},{6,0},{1,3},{3,5},{5,7},{7,1},{8,10},{10,12},{12... | collective-permute-start | bytes 3538952 | tf_op jit(solution)/shard_map/ppermute | solution.py:19
  13.9 30.9 %copy-start.11 = (s32[16]{0:T(128)S(1)}, s32[16]{0:T(128)}, u32[]{:S(2)}) copy-start(s32[16]{0:T(128)} %param.17) | copy-start | bytes 196
  13.9 31.4 %copy-start.12 = (s32[16]{0:T(128)S(1)}, s32[16]{0:T(128)}, u32[]{:S(2)}) copy-start(s32[16]{0:T(128)} %param.18) | copy-start | bytes 196
  13.9 33.2 %copy-start.9 = (s32[16,16]{1,0:T(8,128)S(1)}, s32[16,16]{1,0:T(8,128)}, u32[]{:S(2)}) copy-start(s32[16,16]{1,0:T(8,128)} %param.19) | copy-start | bytes 3076
  13.9 33.3 %copy-start.17 = (f32[2,128]{1,0:T(2,128)S(1)}, f32[2,128]{1,0:T(2,128)}, u32[]{:S(2)}) copy-start(f32[2,128]{1,0:T(2,128)} %param.15) | copy-start | bytes 3076
  14.0 2.2 collective-permute-start.9
  41.6 181.0 %all-gather.10.cloned.1.call-start = ((), (), s32[]{:S(2)}) async-start(), calls=%async_computation.3 | async-start | bytes 4456448 | tf_op jit(solution)/shard_map/all_gather | solution.py:123
  41.7 34.3 %collective-permute-start = (bf16[72,8192]{1,0:T(8,128)(2,1)}, bf16[72,8192]{1,0:T(8,128)(2,1)}, u32[]{:S(2)}, u32[]{:S(2)}) collective-permute-start(bf16[72,8192]{1,0:T(8,128)(2,1)} %get-tuple-element.15), channel_id=1, source_target_pairs={{0,1},{1,0},{2,3},{3,2},{4,5},{5,4},{6,7},{7,6},{8,9},{9,8},{10,11... | collective-permute-start | bytes 3538952 | tf_op jit(solution)/shard_map/ppermute | solution.py:23
  43.3 27.9 %collective-permute-start.4 = (bf16[72,8192]{1,0:T(8,128)(2,1)}, bf16[72,8192]{1,0:T(8,128)(2,1)S(1)}, u32[]{:S(2)}, u32[]{:S(2)}) collective-permute-start(bf16[72,8192]{1,0:T(8,128)(2,1)} %get-tuple-element.15), channel_id=1, source_target_pairs={{0,6},{2,0},{4,2},{6,4},{1,7},{3,1},{5,3},{7,5},{8,14},{10,8},{12,... | collective-permute-start | bytes 3538952 | tf_op jit(solution)/shard_map/ppermute | solution.py:19
  51.8 27.7 %collective-permute-start.3 = (bf16[72,4096]{1,0:T(8,128)(2,1)}, bf16[72,4096]{1,0:T(8,128)(2,1)S(1)}, u32[]{:S(2)}, u32[]{:S(2)}) collective-permute-start(bf16[72,4096]{1,0:T(8,128)(2,1)} %slice.326), channel_id=1, source_target_pairs={{0,2},{2,4},{4,6},{6,0},{1,3},{3,5},{5,7},{7,1},{8,10},{10,12},{12... | collective-permute-start | bytes 1769480 | tf_op jit(solution)/shard_map/ppermute | solution.py:19
  72.1 14.9 %collective-permute-start.5 = (bf16[72,4096]{1,0:T(8,128)(2,1)}, bf16[72,4096]{1,0:T(8,128)(2,1)S(1)}, u32[]{:S(2)}, u32[]{:S(2)}) collective-permute-start(bf16[72,4096]{1,0:T(8,128)(2,1)} %slice.327), channel_id=1, source_target_pairs={{0,6},{2,0},{4,2},{6,4},{1,7},{3,1},{5,3},{7,5},{8,14},{10,8},{12,... | collective-permute-start | bytes 1769480 | tf_op jit(solution)/shard_map/ppermute | solution.py:19
  74.8 14.2 %collective-permute-start.2 = (bf16[72,8192]{1,0:T(8,128)(2,1)S(1)}, bf16[72,8192]{1,0:T(8,128)(2,1)S(1)}, u32[]{:S(2)}, u32[]{:S(2)}) collective-permute-start(bf16[72,8192]{1,0:T(8,128)(2,1)S(1)} %collective-permute-done.1), channel_id=1, source_target_pairs={{0,1},{1,0},{2,3},{3,2},{4,5},{5,4},{6,7},{7,6},{8,9},{9,8},{10,11... | collective-permute-start | bytes 3538952 | tf_op jit(solution)/shard_map/ppermute | solution.py:23
  75.9 18.1 %collective-permute-start.7 = (bf16[72,8192]{1,0:T(8,128)(2,1)S(1)}, bf16[72,8192]{1,0:T(8,128)(2,1)S(1)}, u32[]{:S(2)}, u32[]{:S(2)}) collective-permute-start(bf16[72,8192]{1,0:T(8,128)(2,1)S(1)} %collective-permute-done.4), channel_id=1, source_target_pairs={{0,1},{1,0},{2,3},{3,2},{4,5},{5,4},{6,7},{7,6},{8,9},{9,8},{10,11... | collective-permute-start | bytes 3538952 | tf_op jit(solution)/shard_map/ppermute | solution.py:23
  87.1 4.7 %collective-permute-start.6 = (bf16[72,8192]{1,0:T(8,128)(2,1)S(1)}, bf16[72,8192]{1,0:T(8,128)(2,1)S(1)}, u32[]{:S(2)}, u32[]{:S(2)}) collective-permute-start(bf16[72,8192]{1,0:T(8,128)(2,1)S(1)} %pad_maximum_fusion), channel_id=1, source_target_pairs={{0,1},{1,0},{2,3},{3,2},{4,5},{5,4},{6,7},{7,6},{8,9},{9,8},{10,11... | collective-permute-start | bytes 3538952 | tf_op jit(solution)/shard_map/ppermute | solution.py:23
  95.1 21.1 %copy-start.15 = (f32[128]{0:T(128)S(1)}, f32[128]{0:T(128)}, u32[]{:S(2)}) copy-start(f32[128]{0:T(128)} %get-tuple-element.107) | copy-start | bytes 1540
  95.1 22.4 %copy-start.16 = (f32[512]{0:T(512)S(1)}, f32[512]{0:T(512)}, u32[]{:S(2)}) copy-start(f32[512]{0:T(512)} %param.14) | copy-start | bytes 6148
  132.3 32.1 %all-to-all-start = ((bf16[16,72,512]{2,1,0:T(8,128)(2,1)}), bf16[16,72,512]{2,1,0:T(8,128)(2,1)S(1)}, u32[]{:S(2)}, u32[]{:S(2)}) async-start(bf16[16,72,512]{2,1,0:T(8,128)(2,1)} %bitcast.10), calls=%async_computation | async-start | bytes 2359296 | tf_op jit(solution)/shard_map/all_to_all | solution.py:143
  165.4 17.4 %copy-start.21 = (bf16[576,512]{1,0:T(8,128)(2,1)}, bf16[576,512]{1,0:T(8,128)(2,1)S(1)}, u32[]{:S(2)}) copy-start(bf16[576,512]{1,0:T(8,128)(2,1)S(1)} %fusion.15) | copy-start | bytes 1769476
  165.4 4.1 %collective-permute-start.8 = (bf16[576,512]{1,0:T(8,128)(2,1)S(1)}, bf16[576,512]{1,0:T(8,128)(2,1)S(1)}, u32[]{:S(2)}, u32[]{:S(2)}) collective-permute-start(bf16[576,512]{1,0:T(8,128)(2,1)S(1)} %fusion.15), channel_id=1, source_target_pairs={{0,1},{1,0},{2,3},{3,2},{4,5},{5,4},{6,7},{7,6},{8,9},{9,8},{10,11... | collective-permute-start | bytes 1769480 | tf_op jit(solution)/shard_map/ppermute | solution.py:23
  169.5 5.9 %copy-start.23 = (bf16[576,512]{1,0:T(8,128)(2,1)}, bf16[576,512]{1,0:T(8,128)(2,1)S(1)}, u32[]{:S(2)}) copy-start(bf16[576,512]{1,0:T(8,128)(2,1)S(1)} %collective-permute-done.8) | copy-start | bytes 1769476
  176.7 60.6 %collective-permute-start.10 = (bf16[144,1024]{1,0:T(8,128)(2,1)}, bf16[144,1024]{1,0:T(8,128)(2,1)S(1)}, u32[]{:S(2)}, u32[]{:S(2)}) collective-permute-start(bf16[144,1024]{1,0:T(8,128)(2,1)} %get-tuple-element.18), channel_id=1, source_target_pairs={{0,2},{2,4},{4,6},{6,0},{1,3},{3,5},{5,7},{7,1},{8,10},{10,12},{12... | collective-permute-start | bytes 884744 | tf_op jit(solution)/shard_map/ppermute | solution.py:19
  184.9 52.7 %collective-permute-start.12 = (bf16[144,1024]{1,0:T(8,128)(2,1)}, bf16[144,1024]{1,0:T(8,128)(2,1)S(1)}, u32[]{:S(2)}, u32[]{:S(2)}) collective-permute-start(bf16[144,1024]{1,0:T(8,128)(2,1)} %get-tuple-element.21), channel_id=1, source_target_pairs={{0,6},{2,0},{4,2},{6,4},{1,7},{3,1},{5,3},{7,5},{8,14},{10,8},{12,... | collective-permute-start | bytes 884744 | tf_op jit(solution)/shard_map/ppermute | solution.py:19
  229.9 10.6 %collective-permute-start.15 = (bf16[144,1024]{1,0:T(8,128)(2,1)S(1)}, bf16[144,1024]{1,0:T(8,128)(2,1)S(1)}, u32[]{:S(2)}, u32[]{:S(2)}) collective-permute-start(bf16[144,1024]{1,0:T(8,128)(2,1)S(1)} %get-tuple-element.22), channel_id=1, source_target_pairs={{0,2},{2,4},{4,6},{6,0},{1,3},{3,5},{5,7},{7,1},{8,10},{10,12},{12... | collective-permute-start | bytes 884744 | tf_op jit(solution)/shard_map/ppermute | solution.py:19
  235.6 7.9 %collective-permute-start.17 = (bf16[144,1024]{1,0:T(8,128)(2,1)S(1)}, bf16[144,1024]{1,0:T(8,128)(2,1)S(1)}, u32[]{:S(2)}, u32[]{:S(2)}) collective-permute-start(bf16[144,1024]{1,0:T(8,128)(2,1)S(1)} %get-tuple-element.25), channel_id=1, source_target_pairs={{0,6},{2,0},{4,2},{6,4},{1,7},{3,1},{5,3},{7,5},{8,14},{10,8},{12,... | collective-permute-start | bytes 884744 | tf_op jit(solution)/shard_map/ppermute | solution.py:19
  237.5 14.9 %collective-permute-start.11 = (bf16[144,2048]{1,0:T(8,128)(2,1)S(1)}, bf16[144,2048]{1,0:T(8,128)(2,1)S(1)}, u32[]{:S(2)}, u32[]{:S(2)}) collective-permute-start(bf16[144,2048]{1,0:T(8,128)(2,1)S(1)} %pad_maximum_fusion.5), channel_id=1, source_target_pairs={{0,2},{2,4},{4,6},{6,0},{1,3},{3,5},{5,7},{7,1},{8,10},{10,12},{12... | collective-permute-start | bytes 1769480 | tf_op jit(solution)/shard_map/ppermute | solution.py:19
  237.7 18.3 %collective-permute-start.13 = (bf16[144,2048]{1,0:T(8,128)(2,1)S(1)}, bf16[144,2048]{1,0:T(8,128)(2,1)S(1)}, u32[]{:S(2)}, u32[]{:S(2)}) collective-permute-start(bf16[144,2048]{1,0:T(8,128)(2,1)S(1)} %pad_maximum_fusion.6), channel_id=1, source_target_pairs={{0,6},{2,0},{4,2},{6,4},{1,7},{3,1},{5,3},{7,5},{8,14},{10,8},{12,... | collective-permute-start | bytes 1769480 | tf_op jit(solution)/shard_map/ppermute | solution.py:19
  240.6 24.4 %collective-permute-start.16 = (bf16[144,2048]{1,0:T(8,128)(2,1)S(1)}, bf16[144,2048]{1,0:T(8,128)(2,1)S(1)}, u32[]{:S(2)}, u32[]{:S(2)}) collective-permute-start(bf16[144,2048]{1,0:T(8,128)(2,1)S(1)} %pad_maximum_fusion.7), channel_id=1, source_target_pairs={{0,2},{2,4},{4,6},{6,0},{1,3},{3,5},{5,7},{7,1},{8,10},{10,12},{12... | collective-permute-start | bytes 1769480 | tf_op jit(solution)/shard_map/ppermute | solution.py:19
  243.6 25.2 %collective-permute-start.18 = (bf16[144,2048]{1,0:T(8,128)(2,1)S(1)}, bf16[144,2048]{1,0:T(8,128)(2,1)S(1)}, u32[]{:S(2)}, u32[]{:S(2)}) collective-permute-start(bf16[144,2048]{1,0:T(8,128)(2,1)S(1)} %pad_maximum_fusion.8), channel_id=1, source_target_pairs={{0,6},{2,0},{4,2},{6,4},{1,7},{3,1},{5,3},{7,5},{8,14},{10,8},{12,... | collective-permute-start | bytes 1769480 | tf_op jit(solution)/shard_map/ppermute | solution.py:19
  257.5 13.5 %collective-permute-start.14 = (bf16[72,2048]{1,0:T(8,128)(2,1)S(1)}, bf16[72,2048]{1,0:T(8,128)(2,1)S(1)}, u32[]{:S(2)}, u32[]{:S(2)}) collective-permute-start(bf16[72,2048]{1,0:T(8,128)(2,1)S(1)} %broadcast_select_fusion.2), channel_id=1, source_target_pairs={{0,1},{1,0},{2,3},{3,2},{4,5},{5,4},{6,7},{7,6},{8,9},{9,8},{10,11... | collective-permute-start | bytes 884744 | tf_op jit(solution)/shard_map/ppermute | solution.py:23
  269.0 3.2 %collective-permute-start.19 = (bf16[72,2048]{1,0:T(8,128)(2,1)S(1)}, bf16[72,2048]{1,0:T(8,128)(2,1)S(1)}, u32[]{:S(2)}, u32[]{:S(2)}) collective-permute-start(bf16[72,2048]{1,0:T(8,128)(2,1)S(1)} %broadcast_select_fusion), channel_id=1, source_target_pairs={{0,1},{1,0},{2,3},{3,2},{4,5},{5,4},{6,7},{7,6},{8,9},{9,8},{10,11... | collective-permute-start | bytes 884744 | tf_op jit(solution)/shard_map/ppermute | solution.py:23
  (18 other events, 49.6 us)
Sparse Core Ops, SparseCore 0:
  9.8 93.3 all-gather.5
  105.3 63.9 all-gather.7
  171.5 51.1 all-gather.9
